TPU v7x, 32 devices: a whole 2x2x4 slice. The times are simulated.
32 devices in a mesh: clip: 4 (over y, core), row: 2 (over x), src: 4 (over z).
Axes of the slice: x: 2, y: 2, z: 4, core: 2. Of those that a mesh axis runs over, the one named last changes fastest.
Arguments:
- mask_clip: bfloat16 [16384, 4096], P(('clip', 'row'), 'src'), parts along dimension 0, may hold values from -6 to 6
- source_shifts: int32 [16, 2], P('src'), may hold values from -64 to 64
- source_weights: int32 [16], P('src'), may hold values from 1 to 8
Outputs:
- intensity: float32 [4096, 1024], P(('clip', 'row', 'src')), parts along dimension 0
There are 4 independent parts, one for each index of `clip`. A program takes and returns all parts, laid end to end along the dimension named above; an argument that names none is the same for every part. Nothing has to cross between parts.
All inputs are finite; a program needn't handle non-finite values.
Results may differ from a plain program's by a relative error of at most 0.0052.
Values may be sent and summed in bfloat16 or wider, within the bound.
A program may use at most 64 MiB of HBM per device.

v0:
```python
import math

import jax
import jax.numpy as jnp
from jax import lax
from jax.sharding import PartitionSpec as P

NM = 4096
P_SIZE = 256
NI = 1024


def twiddles(positions, length, scaling):
    frequency = jnp.arange(P_SIZE, dtype=jnp.int32) - P_SIZE // 2
    product = jnp.mod(positions[:, None] * frequency[None, :], length)
    angles = product.astype(jnp.float32) * jnp.float32(2.0 * math.pi / length)
    return (jnp.cos(angles) * jnp.float32(scaling), jnp.sin(angles) * jnp.float32(scaling))


def tile_spectrum(mask_tile, row_first, col_first):
    row_index = row_first + jnp.arange(mask_tile.shape[0], dtype=jnp.int32)
    col_index = col_first + jnp.arange(mask_tile.shape[1], dtype=jnp.int32)
    col_cos, col_sin = twiddles(col_index, NM, 1.0 / math.sqrt(NM))
    col_table = jnp.concatenate([col_cos, -col_sin], 1).astype(jnp.bfloat16)
    half_way = jnp.dot(mask_tile, col_table, preferred_element_type=jnp.float32).astype(
        jnp.bfloat16
    )
    row_cos, row_sin = twiddles(row_index, NM, 1.0 / math.sqrt(NM))
    row_table = jnp.concatenate([row_cos, row_sin], 1).T.astype(jnp.bfloat16)
    blocks = jnp.dot(row_table, half_way, preferred_element_type=jnp.float32)
    real_part = blocks[:P_SIZE, :P_SIZE] + blocks[P_SIZE:, P_SIZE:]
    imag_part = blocks[:P_SIZE, P_SIZE:] - blocks[P_SIZE:, :P_SIZE]
    return jnp.stack([real_part, imag_part])


def build_left(image_rows):
    row_cos, row_sin = twiddles(image_rows, NI, 1.0 / math.sqrt(P_SIZE))
    return jnp.concatenate([row_cos, row_sin], 0).astype(jnp.bfloat16)


def build_right():
    col_cos, col_sin = twiddles(jnp.arange(NI, dtype=jnp.int32), NI, 1.0 / math.sqrt(P_SIZE))
    upper = jnp.concatenate([col_cos.T, col_sin.T], 1)
    lower = jnp.concatenate([-col_sin.T, col_cos.T], 1)
    return jnp.concatenate([upper, lower], 0).astype(jnp.bfloat16)


def source_image(spectrum, shift_pair, weight, left_table, right_table):
    frequency = jnp.arange(P_SIZE, dtype=jnp.int32) - P_SIZE // 2
    along_rows = frequency + shift_pair[0]
    along_cols = frequency + shift_pair[1]
    radius = P_SIZE // 4
    inside = (
        along_rows[:, None] * along_rows[:, None] + along_cols[None, :] * along_cols[None, :]
        <= radius * radius
    )
    pupil_mask = inside.astype(jnp.bfloat16)
    passed = jnp.concatenate([spectrum[0] * pupil_mask, spectrum[1] * pupil_mask], 1)
    blocks = jnp.dot(left_table, passed, preferred_element_type=jnp.float32)
    row_count = left_table.shape[0] // 2
    k_real = blocks[:row_count, :P_SIZE] - blocks[row_count:, P_SIZE:]
    k_imag = blocks[:row_count, P_SIZE:] + blocks[row_count:, :P_SIZE]
    partial_value = jnp.concatenate([k_real, k_imag], 1).astype(jnp.bfloat16)
    field_pair = jnp.dot(partial_value, right_table, preferred_element_type=jnp.float32)
    field_real = field_pair[:, :NI]
    field_imag = field_pair[:, NI:]
    return weight.astype(jnp.float32) * (field_real * field_real + field_imag * field_imag)


def image_rows_sum(spectrum, image_rows, all_shifts, all_weights, right_table):
    left_table = build_left(image_rows)

    def add_source(running, source_item):
        shift_pair, weight = source_item
        return (running + source_image(spectrum, shift_pair, weight, left_table, right_table), None)

    summed, _ = lax.scan(
        add_source, jnp.zeros((image_rows.shape[0], NI), jnp.float32), (all_shifts, all_weights)
    )
    return summed


def body(mask_clip, source_shifts, source_weights):
    row_id = lax.axis_index("row")
    src_id = lax.axis_index("src")
    strip_rows = mask_clip.shape[0]
    strip_cols = mask_clip.shape[1]
    partial_value = tile_spectrum(mask_clip, row_id * strip_rows, src_id * strip_cols)
    spectrum = lax.psum(partial_value, ("row", "src")).astype(jnp.bfloat16)
    right_table = build_right()
    image_strip = NI // lax.axis_size("row")
    rows_dev = image_strip // lax.axis_size("src")
    sources = source_shifts.shape[0] * lax.axis_size("src")
    image_rows = row_id * image_strip + jnp.arange(rows_dev * lax.axis_size("src"), dtype=jnp.int32)
    summed = lax.psum_scatter(
        image_rows_sum(spectrum, image_rows, source_shifts, source_weights, right_table),
        "src",
        scatter_dimension=0,
        tiled=True,
    )
    return summed / jnp.float32(sources)


def solution(mesh):
    placed = (P(("clip", "row"), "src"), P("src", None), P("src"))
    return jax.shard_map(
        body, mesh=mesh, in_specs=placed, out_specs=P(("clip", "row", "src"), None), check_vma=False
    )
```

profile of v0, /device:TPU:0, one launch (start us, length us, event | category | flops | bytes accessed | tf_op | source)
XLA Modules:
  0.0 174.6 jit_solution(12972776028633526755)
XLA Ops:
  6.5 0.0 reduce-scatter.2.cloned.1.call-start
  6.6 5.7 %fusion.35 = (bf16[256,1024]{1,0:T(8,128)(2,1)S(1)}, bf16[256,1024]{1,0:T(8,128)(2,1)}, bf16[256,1024]{1,0:T(8,128)(2,1)}) fusion(s32[256]{0:T(256)S(1)} %iota_add_fusion.4), kind=kLoop, calls=%fused_computation.70 | loop fusion | flops 5242880 | bytes 1573888 | tf_op jit(solution)/shard_map/convert.7
  12.3 3.2 %multiply_convert_fusion.5 = (bf16[512,256]{1,0:T(8,128)(2,1)}, bf16[512,256]{1,0:T(8,128)(2,1)}) fusion(s32[256]{0:T(256)S(1)} %iota_add_fusion.4, s32[512]{0:T(512)S(1)} %iota_add_fusion.3), kind=kLoop, calls=%fused_computation.79 | loop fusion | flops 2359296 | bytes 527360 | tf_op jit(solution)/shard_map/convert.8
  15.5 5.6 %multiply_convert_fusion.3 = (bf16[1024,256]{1,0:T(8,128)(2,1)S(1)}, bf16[1024,256]{1,0:T(8,128)(2,1)}) fusion(s32[256]{0:T(256)S(1)} %iota_add_fusion.4, s32[1024]{0:T(1024)S(1)} %iota_add_fusion.2), kind=kLoop, calls=%fused_computation.65 | loop fusion | flops 4980736 | bytes 1053696 | tf_op jit(solution)/shard_map/convert.10
  21.1 10.2 %multiply_convert_fusion.1 = (bf16[2048,256]{1,0:T(8,128)(2,1)}, bf16[2048,256]{1,0:T(8,128)(2,1)}) fusion(s32[256]{0:T(256)S(1)} %iota_add_fusion.4, s32[2048]{0:T(1024)S(1)} %iota_add_fusion.1), kind=kLoop, calls=%fused_computation.41 | loop fusion | flops 9437184 | bytes 2106368 | tf_op jit(solution)/shard_map/convert.12
  31.3 7.5 %fusion.19 = f32[512,512]{1,0:T(8,128)} fusion(bf16[2048,256]{1,0:T(8,128)(2,1)} %get-tuple-element.144, bf16[2048,256]{1,0:T(8,128)(2,1)} %get-tuple-element.143, bf16[2048,1024]{1,0:T(8,128)(2,1)} %param.5, bf16[1024,256]{1,0:T(8,128)(2,1)} %get-tuple-element.146, bf16[1024,256]{1,0:T(8,128)(2,1)S(1)} %get-tuple-element.145), kind=kOutput, calls=%fused_computation.35 | convolution fusion | flops 3228565504 | bytes 8388608 | tf_op jit(solution)/shard_map/dot_general | solution.py:30
  38.8 1.3 fusion.42
  40.1 49.4 %all-reduce.1 = bf16[2,256,256]{2,1,0:T(8,128)(2,1)S(1)} all-reduce(f32[2,256,256]{2,1,0:T(8,128)S(1)} %pad_maximum_fusion), channel_id=1, replica_groups=mesh['clip'=4,'row'=2,'src'=4] {'row','src'}, use_global_device_ids=true, to_apply=%region_0.1 | all-reduce | flops 131072 | bytes 786432 | tf_op jit(solution)/shard_map/psum | solution.py:89
  89.5 1.1 pad_maximum_fusion.1
  90.6 0.0 copy-start.2
  90.6 0.0 copy-start.3
  90.6 2.9 %maximum_maximum_fusion = bf16[512,2048]{1,0:T(8,128)(2,1)} fusion(bf16[256,1024]{1,0:T(8,128)(2,1)} %get-tuple-element.151, bf16[256,1024]{1,0:T(8,128)(2,1)} %get-tuple-element.150, bf16[256,1024]{1,0:T(8,128)(2,1)S(1)} %get-tuple-element.149), kind=kLoop, calls=%fused_computation.39 | loop fusion | flops 8388608 | bytes 3670016 | tf_op jit(solution)/shard_map/concatenate | solution.py:45
  93.5 0.0 copy-done.2
  93.5 0.0 copy-done.3
  93.5 29.0 %while.13 = (s32[]{:T(128)}, f32[512,1024]{1,0:T(8,128)S(1)}, s32[4]{0:T(128)S(1)}, s32[4,2]{0,1:T(2,128)S(1)}, bf16[2,256,256]{2,1,0:T(8,128)(2,1)S(1)}, /*inde...) while((s32[]{:T(128)}, f32[512,1024]{1,0:T(8,128)S(1)}, ...), condition=%wide.region_2.3_spmd.clone, body=%wide.region_1.2_spmd.clone.sunk | while | flops 1347683584 | bytes 29626572 | solution.py:77
  93.5 0.6 dynamic_slice.20
  94.7 0.1 constant_dynamic-slice_fusion.2
  94.8 0.5 fusion.62
  95.3 1.2 add_multiply_fusion.3
  96.5 0.1 fusion.63
  96.6 0.0 copy-start.1
  96.7 0.5 convolution_bitcast_fusion.2
  97.1 0.2 fusion.64
  97.3 0.9 copy-done.1
  98.2 1.3 fusion.65
  99.5 1.2 fusion.66
  100.7 0.6 dynamic_slice.20
  102.0 0.1 constant_dynamic-slice_fusion.2
  102.1 0.5 fusion.62
  102.6 1.2 add_multiply_fusion.3
  103.8 0.1 fusion.63
  103.9 0.0 copy-start.1
  103.9 0.5 convolution_bitcast_fusion.2
  104.4 0.2 fusion.64
  104.6 0.9 copy-done.1
  105.5 1.3 fusion.65
  106.8 1.2 fusion.66
  108.0 0.6 dynamic_slice.20
  109.3 0.1 constant_dynamic-slice_fusion.2
  109.3 0.5 fusion.62
  109.8 1.2 add_multiply_fusion.3
  111.1 0.1 fusion.63
  111.2 0.0 copy-start.1
  111.2 0.5 convolution_bitcast_fusion.2
  111.7 0.2 fusion.64
  111.8 0.9 copy-done.1
  112.8 1.3 fusion.65
  114.1 1.2 fusion.66
  115.3 0.6 dynamic_slice.20
  116.5 0.1 constant_dynamic-slice_fusion.2
  116.6 0.5 fusion.62
  117.1 1.2 add_multiply_fusion.3
  118.3 0.1 fusion.63
  118.4 0.0 copy-start.1
  118.4 0.5 convolution_bitcast_fusion.2
  118.9 0.2 fusion.64
  119.1 0.9 copy-done.1
  120.0 1.3 fusion.65
  121.3 1.2 fusion.66
  122.5 0.0 copy-start
  122.6 1.3 copy-done
  123.9 0.0 reduce-scatter.2.cloned.1.call-update
  123.9 41.9 %reduce-scatter.2.cloned.1.call-done = f32[128,1024]{1,0:T(8,128)} async-done(((f32[512,1024]{1,0:T(8,128)}), f32[128,1024]{1,0:T(8,128)}) %reduce-scatter.2.cloned.1.call-update) | async-done | bytes 524304 | tf_op jit(solution)/shard_map/reduce_scatter | solution.py:95
  165.8 1.9 %broadcast_multiply_fusion = f32[128,1024]{1,0:T(8,128)} fusion(f32[128,1024]{1,0:T(8,128)} %reduce-scatter.2.cloned.1.call-done), kind=kLoop, calls=%fused_computation.84 | loop fusion | flops 131072 | bytes 1048576 | tf_op jit(solution)/shard_map/div | solution.py:101
  (6 shorter events, 0.1 us)
Async XLA Ops:
  6.5 159.3 %reduce-scatter.2.cloned.1.call-start = ((), (), s32[]{:S(2)}) async-start(), calls=%async_computation.1 | async-start | bytes 2621440 | tf_op jit(solution)/shard_map/reduce_scatter | solution.py:95
  90.6 2.9 %copy-start.2 = (s32[4,2]{0,1:T(2,128)S(1)}, s32[4,2]{0,1:T(2,128)}, u32[]{:S(2)}) copy-start(s32[4,2]{0,1:T(2,128)} %param.6) | copy-start | bytes 100
  90.6 2.9 %copy-start.3 = (s32[4]{0:T(128)S(1)}, s32[4]{0:T(128)}, u32[]{:S(2)}) copy-start(s32[4]{0:T(128)} %param.7) | copy-start | bytes 52
  96.6 1.6 copy-start.1
  103.9 1.6 copy-start.1
  111.2 1.6 copy-start.1
  118.4 1.6 copy-start.1
  122.5 1.3 copy-start
Sparse Core Ops, SparseCore 0:
  124.0 41.7 reduce-scatter.1
where the time goes:
time: 175 us
  blocking collectives  49.4 us (28%)
  other arithmetic  42.6 us (24%)
  waiting for transfers between devices  42 us (24%)
  matrix products  14.5 us (8%)
  between operations  13.5 us (8%)
  local copies, waits for them, and re-layouts  9.76 us (6%)
  loops' own time  2.81 us (2%)
    psum x1, blocking collectives, body(): spectrum = lax.psum(partial_value, ('row', 'src')).astype(jnp.bfloat16)  49.4 us
    reduce_scatter x1, waiting for transfers between devices, body(): lax.psum_scatter(image_rows_sum(spectrum, image_rows, source_shifts, sour...  41.9 us
    another operation x8, other arithmetic  25.4 us
    dot_general x1, matrix products, tile_spectrum(): blocks = jnp.dot(row_table, half_way, preferred_element_type=jnp.float32)  7.46 us
    dot_general x4, matrix products, source_image(): jnp.dot(partial_value, right_table, preferred_element_type=jnp.float32)  5.15 us
    add x4, other arithmetic, add_source(): running + source_image(spectrum, shift_pair, weight, left_table, right_ta...  4.83 us
    mul x4, other arithmetic, source_image(): along_cols[None, :] * along_cols[None, :]  4.79 us
    while x8, local copies, waits for them, and re-layouts  3.71 us
  transfers between devices with their start and end apart: 1, of which 1 were waited for; matrix products, arithmetic and copies ran while one was open for 0% of the time, Pallas kernels for 0%

commit v1 on v0

v1 whole, which is shorter than its diff:
```python
import functools
import math

import jax
import jax.numpy as jnp
import ml_dtypes
import numpy as np
from jax import lax
from jax.experimental import pallas as pl
from jax.experimental.pallas import tpu as pltpu
from jax.sharding import PartitionSpec as P

P_SIZE = 256
NI = 1024
COARSE = 512
MESH = pl.DeviceIdType.MESH
BF16 = ml_dtypes.bfloat16


def twiddles(positions, length, scaling):
    frequency = np.arange(P_SIZE) - P_SIZE // 2
    angles = np.mod(positions[:, None] * frequency[None, :], length) * (2.0 * math.pi / length)
    return np.cos(angles) * scaling, np.sin(angles) * scaling


@functools.lru_cache(maxsize=None)
def forward_table(length):
    cos, sin = twiddles(np.arange(length), length, 1.0 / math.sqrt(length))
    return np.concatenate([cos, sin], 1).astype(np.float32).astype(BF16)


@functools.lru_cache(maxsize=None)
def inverse_tables(row_blocks):
    cos, sin = twiddles(np.arange(NI), NI, 1.0 / math.sqrt(P_SIZE))
    cols = np.concatenate([cos, sin], 1)[:: NI // COARSE]
    block = NI // row_blocks
    rows = np.stack(
        [
            np.block([[c.T, s.T], [-s.T, c.T]])
            for c, s in zip(cos.reshape(-1, block, P_SIZE), sin.reshape(-1, block, P_SIZE))
        ]
    )
    band = P_SIZE // 2
    u = np.arange(-COARSE, COARSE + 1)
    ramp = np.clip((np.abs(u) - band) / (COARSE - 2 * band), 0.0, 1.0)
    gain = 0.5 + 0.5 * np.cos(math.pi * ramp)
    offset = np.arange(NI)
    kernel = (gain[None, :] * np.cos(2 * math.pi * offset[:, None] * u[None, :] / NI)).sum(1) / COARSE
    step = NI // COARSE
    spread = kernel[np.mod(np.arange(NI)[None, :] - step * np.arange(COARSE)[:, None], NI)]
    high = spread.astype(np.float32).astype(BF16)
    low = (spread - high.astype(np.float64)).astype(np.float32).astype(BF16)
    as_bf16 = lambda x: x.astype(np.float32).astype(BF16)
    return as_bf16(rows), as_bf16(cols), high, low


def spectrum_kernel(
    n_row, n_src, chunks,
    mask_hbm, col_hbm, row_hbm, own_ref,
    spec_ref, points_ref,
    mask, col, row, half, part, send, arrived,
    load_sem, rs_send, rs_recv, ag_send, ag_recv, pt_send, pt_recv,
):
    n = n_row * n_src
    row_id, src_id = lax.axis_index("row"), lax.axis_index("src")
    me = row_id * n_src + src_id
    rows, cols = mask.shape
    piece = rows // chunks
    per = P_SIZE // n

    loads = [
        pltpu.make_async_copy(
            col_hbm.at[pl.ds(pl.multiple_of(src_id * cols, cols), cols)], col, load_sem.at[0]
        )
    ]
    for i in range(chunks):
        loads.append(
            pltpu.make_async_copy(
                mask_hbm.at[pl.ds(i * piece, piece)], mask.at[pl.ds(i * piece, piece)],
                load_sem.at[1 + i],
            )
        )
    loads.append(
        pltpu.make_async_copy(
            row_hbm.at[:, pl.ds(pl.multiple_of(row_id * rows, rows), rows)], row,
            load_sem.at[1 + chunks],
        )
    )
    for load in loads:
        load.start()

    def partner(k):
        other = lax.rem(me + k, n)
        return other, {"row": other // n_src, "src": lax.rem(other, n_src)}

    barrier = pltpu.get_barrier_semaphore()
    for k in range(1, n):
        pl.semaphore_signal(barrier, inc=1, device_id=partner(k)[1], device_id_type=MESH)

    loads[0].wait()
    for i in range(chunks):
        loads[1 + i].wait()
        half[pl.ds(i * piece, piece)] = jnp.dot(
            mask[pl.ds(i * piece, piece)], col[...], preferred_element_type=jnp.float32
        ).astype(jnp.bfloat16)
    loads[-1].wait()
    blocks = jnp.dot(row[...], half[...], preferred_element_type=jnp.float32)
    p = P_SIZE
    part[:, :p] = blocks[:p, :p] - blocks[p:, p:]
    part[:, p:] = -blocks[:p, p:] - blocks[p:, :p]
    send[...] = part[...].astype(jnp.bfloat16)

    pl.semaphore_wait(barrier, n - 1)
    outgoing = []
    for k in range(1, n):
        other, where = partner(k)
        copy = pltpu.make_async_remote_copy(
            src_ref=send.at[pl.ds(pl.multiple_of(other * per, per), per)],
            dst_ref=arrived.at[k],
            send_sem=rs_send.at[k], recv_sem=rs_recv.at[k],
            device_id=where, device_id_type=MESH,
        )
        copy.start()
        outgoing.append(copy)
    point_copies = []
    for k in range(1, n_src):
        copy = pltpu.make_async_remote_copy(
            src_ref=own_ref, dst_ref=points_ref.at[src_id],
            send_sem=pt_send.at[k], recv_sem=pt_recv.at[k],
            device_id={"src": lax.rem(src_id + k, n_src)}, device_id_type=MESH,
        )
        copy.start()
        point_copies.append(copy)
    points_ref[src_id] = own_ref[...]

    mine = pl.ds(pl.multiple_of(me * per, per), per)
    total = part[mine]
    for k, copy in enumerate(outgoing, 1):
        copy.wait_recv()
        total = total + arrived[k].astype(jnp.float32)
    spec_ref[mine] = total.astype(jnp.bfloat16)
    gathered = []
    for k in range(1, n):
        copy = pltpu.make_async_remote_copy(
            src_ref=spec_ref.at[mine], dst_ref=spec_ref.at[mine],
            send_sem=ag_send.at[k], recv_sem=ag_recv.at[k],
            device_id=partner(k)[1], device_id_type=MESH,
        )
        copy.start()
        gathered.append(copy)
    for copy in point_copies + gathered:
        copy.wait_recv()
    for copy in outgoing + point_copies + gathered:
        copy.wait_send()


def image_kernel(spec_ref, points, rows_hbm, col_ref, high_ref, low_ref, out_ref, rows, turned, halves, total, sem):
    n_src = lax.axis_size("src")
    me = lax.axis_index("row") * n_src + lax.axis_index("src")
    load = pltpu.make_async_copy(rows_hbm.at[me], rows, sem.at[0])
    load.start()
    p = P_SIZE
    block = out_ref.shape[0]
    per = points.shape[1]
    sources = points.shape[0] * per
    turned[:, :p] = spec_ref[:, :p].astype(jnp.float32).T.astype(jnp.bfloat16)
    turned[:, p:] = spec_ref[:, p:].astype(jnp.float32).T.astype(jnp.bfloat16)
    along_rows = lax.broadcasted_iota(jnp.int32, (p, p), 1) - p // 2
    along_cols = lax.broadcasted_iota(jnp.int32, (p, p), 0) - p // 2
    radius = p // 4
    load.wait()

    def first(s, carry):
        down = along_rows + points[s // per, lax.rem(s, per), 0]
        across = along_cols + points[s // per, lax.rem(s, per), 1]
        inside = down * down + across * across <= radius * radius
        pupil = jnp.where(inside, 1.0, 0.0).astype(jnp.bfloat16)
        passed = jnp.concatenate([turned[:, :p] * pupil, turned[:, p:] * pupil], 1)
        k = jnp.dot(passed, rows[...], preferred_element_type=jnp.float32).astype(jnp.bfloat16)
        halves[s, :p] = k
        halves[s, p:, :block] = -k[:, block:]
        halves[s, p:, block:] = k[:, :block]
        return carry

    lax.fori_loop(0, sources, first, 0, unroll=2)
    total[...] = jnp.zeros_like(total)

    def second(s, carry):
        weight = points[s // per, lax.rem(s, per), 2].astype(jnp.float32) * (1.0 / sources)
        e = jnp.dot(col_ref[...], halves[s], preferred_element_type=jnp.float32)
        total[...] += weight * (e[:, :block] * e[:, :block] + e[:, block:] * e[:, block:])
        return carry

    lax.fori_loop(0, sources, second, 0, unroll=2)
    summed = total[...].T
    top = summed.astype(jnp.bfloat16)
    rest = (summed - top.astype(jnp.float32)).astype(jnp.bfloat16)
    out_ref[...] = (
        jnp.dot(top, high_ref[...], preferred_element_type=jnp.float32)
        + jnp.dot(rest, high_ref[...], preferred_element_type=jnp.float32)
        + jnp.dot(top, low_ref[...], preferred_element_type=jnp.float32)
    )


def body(n_row, n_src, mask_clip, source_shifts, source_weights):
    n = n_row * n_src
    rows, cols = mask_clip.shape
    per = P_SIZE // n
    own = jnp.concatenate([source_shifts, source_weights[:, None]], 1)
    chunks = 4
    vmem = pl.BlockSpec(memory_space=pltpu.VMEM)
    anywhere = pl.BlockSpec(memory_space=pl.ANY)
    spec, points = pl.pallas_call(
        functools.partial(spectrum_kernel, n_row, n_src, chunks),
        out_shape=(
            jax.ShapeDtypeStruct((P_SIZE, 2 * P_SIZE), jnp.bfloat16),
            jax.ShapeDtypeStruct((n_src,) + own.shape, jnp.int32),
        ),
        in_specs=[anywhere, anywhere, anywhere, vmem],
        out_specs=(vmem, vmem),
        scratch_shapes=[
            pltpu.VMEM((rows, cols), jnp.bfloat16),
            pltpu.VMEM((cols, 2 * P_SIZE), jnp.bfloat16),
            pltpu.VMEM((2 * P_SIZE, rows), jnp.bfloat16),
            pltpu.VMEM((rows, 2 * P_SIZE), jnp.bfloat16),
            pltpu.VMEM((P_SIZE, 2 * P_SIZE), jnp.float32),
            pltpu.VMEM((P_SIZE, 2 * P_SIZE), jnp.bfloat16),
            pltpu.VMEM((n, per, 2 * P_SIZE), jnp.bfloat16),
            pltpu.SemaphoreType.DMA((chunks + 2,)),
            pltpu.SemaphoreType.DMA((n,)),
            pltpu.SemaphoreType.DMA((n,)),
            pltpu.SemaphoreType.DMA((n,)),
            pltpu.SemaphoreType.DMA((n,)),
            pltpu.SemaphoreType.DMA((n_src,)),
            pltpu.SemaphoreType.DMA((n_src,)),
        ],
        compiler_params=pltpu.CompilerParams(
            collective_id=0, has_side_effects=True, vmem_limit_bytes=40 * 2**20
        ),
        name="spectrum",
    )(
        mask_clip,
        jnp.asarray(forward_table(n_src * cols)),
        jnp.asarray(np.ascontiguousarray(forward_table(n_row * rows).T)),
        own,
    )
    row_table, col_table, high, low = inverse_tables(n)
    block = NI // n
    sources = n_src * own.shape[0]
    return pl.pallas_call(
        image_kernel,
        out_shape=jax.ShapeDtypeStruct((block, NI), jnp.float32),
        in_specs=[vmem, pl.BlockSpec(memory_space=pltpu.SMEM), anywhere, vmem, vmem, vmem],
        out_specs=vmem,
        scratch_shapes=[
            pltpu.VMEM((2 * P_SIZE, 2 * block), jnp.bfloat16),
            pltpu.VMEM((P_SIZE, 2 * P_SIZE), jnp.bfloat16),
            pltpu.VMEM((sources, 2 * P_SIZE, 2 * block), jnp.bfloat16),
            pltpu.VMEM((COARSE, block), jnp.float32),
            pltpu.SemaphoreType.DMA((1,)),
        ],
        compiler_params=pltpu.CompilerParams(vmem_limit_bytes=40 * 2**20),
        name="image",
    )(spec, points, jnp.asarray(row_table), jnp.asarray(col_table), jnp.asarray(high), jnp.asarray(low))


def solution(mesh):
    placed = (P(("clip", "row"), "src"), P("src", None), P("src"))
    return jax.shard_map(
        functools.partial(body, mesh.shape["row"], mesh.shape["src"]),
        mesh=mesh, in_specs=placed, out_specs=P(("clip", "row", "src"), None), check_vma=False,
    )
```

time: 175 us -> 39.4 us (0.23)
  blocking collectives: 49.4 us -> 0 us
  other arithmetic: 42.6 us -> 0.08 us
  waiting for transfers between devices: 42 us -> 0 us
  Pallas kernels: 0 us -> 30.9 us
  matrix products: 14.5 us -> 0 us
  between operations: 13.5 us -> 0.05 us
  loops' own time: 2.81 us -> 0 us
    psum x1 -> x0, blocking collectives: 49.4 us -> none  [body(): spectrum = lax.psum(partial_value, ('row', 'src')).astype(jnp.bfloat16)]
    reduce_scatter x1 -> x0, waiting for transfers between devices: 41.9 us -> none  [body(): lax.psum_scatter(image_rows_sum(spectrum, image_rows, source_shifts, sour...]
    pallas_call x0 -> x2, Pallas kernels: none -> 30.9 us  [the longest x1 22.5 us: body(): pl.pallas_call(functools.partial(spectrum_kernel, n_row, n_src, chunks),...]
    another operation x10 -> x0, other arithmetic: 26.7 us -> none
    dot_general x9 -> x0, matrix products: 14.5 us -> none  [the longest x1 7.46 us: tile_spectrum(): blocks = jnp.dot(row_table, half_way, preferred_element_type=jnp.float32)]
    unnamed x6 -> x15, local copies, waits for them, and re-layouts: 1.33 us -> 7.34 us
    mul x8 -> x0, other arithmetic: 5.24 us -> none  [the longest x4 4.79 us: source_image(): along_cols[None, :] * along_cols[None, :]]
    add x7 -> x0, other arithmetic: 4.85 us -> none  [the longest x4 4.83 us: add_source(): running + source_image(spectrum, shift_pair, weight, left_table, right_ta...]
  transfers between devices with their start and end apart: 1 -> 0, of which waited for: 1 -> 0; matrix products, arithmetic and copies ran while one was open for 0% -> 0% of each run, Pallas kernels for 0% -> 0%
where the time goes in v1:
time: 39.4 us; the launch traced here: 39.1 us
  Pallas kernels  30.9 us (78%)
  local copies, waits for them, and re-layouts  8.08 us (21%)
    pallas_call x1, Pallas kernels, body(): pl.pallas_call(functools.partial(spectrum_kernel, n_row, n_src, chunks),...  22.5 us
    pallas_call x1, Pallas kernels, body(): pl.pallas_call(image_kernel, out_shape=jax.ShapeDtypeStruct((block, NI),...  8.44 us
    unnamed x15, local copies, waits for them, and re-layouts  7.34 us

profile of v1, /device:TPU:0, one launch (start us, length us, event | category | flops | bytes accessed | tf_op | source)
XLA Modules:
  0.0 39.1 jit_solution(2900031323178348242)
XLA Ops:
  0.0 0.8 %copy.10 = s32[4,2]{1,0:T(4,128)S(1)} copy(s32[4,2]{0,1:T(2,128)} %param.10) | data formatting | bytes 64 | tf_op args[1]
  0.8 0.7 %copy.11 = s32[4,1]{1,0:T(4,128)S(1)} copy(s32[4,1]{0,1:T(1,128)} %bitcast.1) | data formatting | bytes 32 | tf_op jit(solution)/shard_map/broadcast_in_dim | solution.py:209
  1.5 0.1 pad_add_fusion.own_ref
  1.6 0.0 copy-start
  1.6 2.2 %copy-done = bf16[2048,1024]{1,0:T(8,128)(2,1)S(1)} copy-done((bf16[2048,1024]{1,0:T(8,128)(2,1)S(1)}, bf16[2048,1024]{1,0:T(8,128)(2,1)}, u32[]{:S(2)}) %copy-start) | copy-done | bytes 4194328
  3.8 0.0 copy-start.1
  3.8 2.2 %copy-done.1 = bf16[512,4096]{1,0:T(8,128)(2,1)S(1)} copy-done((bf16[512,4096]{1,0:T(8,128)(2,1)S(1)}, bf16[512,4096]{1,0:T(8,128)(2,1)}, u32[]{:S(2)}) %copy-start.1) | copy-done | bytes 4194328
  6.0 0.0 copy-start.2
  6.0 2.2 %copy-done.2 = bf16[4096,512]{1,0:T(8,128)(2,1)S(1)} copy-done((bf16[4096,512]{1,0:T(8,128)(2,1)S(1)}, bf16[4096,512]{1,0:T(8,128)(2,1)}, u32[]{:S(2)}) %copy-start.2) | copy-done | bytes 4194328
  8.1 0.0 copy-start.3
  8.2 0.0 copy-start.4
  8.2 0.0 copy-start.5
  8.2 0.0 copy-start.6
  8.2 22.5 %spectrum.1 = (bf16[256,512]{1,0:T(8,128)(2,1)S(1)}, s32[4,4,3]{2,1,0:T(4,128)S(1)}) custom-call(bf16[2048,1024]{1,0:T(8,128)(2,1)S(1)} %copy-done, bf16[4096,512]{1,0:T(8,128)(2,1)S(1)} %copy-done.2, bf16[512,4096]{1,0:T(8,128)(2,1)S(1)} %copy-done.1, s32[4,3]{1,0:T(4,128)S(1)} %pad_add_fusion.own_ref), custom_call_target="tpu_custom_call" | custom-call | tf_op jit(solution)/shard_map/spectrum/pallas_call | solution.py:213
  30.6 0.0 copy-done.3
  30.6 0.0 copy-done.4
  30.7 0.0 copy-done.5
  30.7 0.0 copy-done.6
  30.7 8.4 %image.1 = f32[128,1024]{1,0:T(8,128)} custom-call(bf16[256,512]{1,0:T(8,128)(2,1)S(1)} %get-tuple-element.7.spec_ref, s32[4,4,3]{2,1,0:T(4,128)S(1)} %get-tuple-element.8.points, bf16[8,512,256]{2,1,0:T(8,128)(2,1)S(1)} %copy-done.3, bf16[512,512]{1,0:T(8,128)(2,1)S(1)} %copy-done.6, bf16[512,1024]{1,0:T(8,128)(2,1)S(1)} %copy-done.5, ...), custom_call_target="tpu_custom_call" | custom-call | tf_op jit(solution)/shard_map/image/pallas_call | solution.py:250
Async XLA Ops:
  1.6 2.2 %copy-start = (bf16[2048,1024]{1,0:T(8,128)(2,1)S(1)}, bf16[2048,1024]{1,0:T(8,128)(2,1)}, u32[]{:S(2)}) copy-start(bf16[2048,1024]{1,0:T(8,128)(2,1)} %mask_hbm.1) | copy-start | bytes 12582916
  3.8 2.2 %copy-start.1 = (bf16[512,4096]{1,0:T(8,128)(2,1)S(1)}, bf16[512,4096]{1,0:T(8,128)(2,1)}, u32[]{:S(2)}) copy-start(bf16[512,4096]{1,0:T(8,128)(2,1)} %constant.13.clone.row_hbm) | copy-start | bytes 12582916
  6.0 2.2 %copy-start.2 = (bf16[4096,512]{1,0:T(8,128)(2,1)S(1)}, bf16[4096,512]{1,0:T(8,128)(2,1)}, u32[]{:S(2)}) copy-start(bf16[4096,512]{1,0:T(8,128)(2,1)} %constant.12.clone.col_hbm) | copy-start | bytes 12582916
  8.1 22.5 %copy-start.3 = (bf16[8,512,256]{2,1,0:T(8,128)(2,1)S(1)}, bf16[8,512,256]{2,1,0:T(8,128)(2,1)}, u32[]{:S(2)}) copy-start(bf16[8,512,256]{2,1,0:T(8,128)(2,1)} %constant.14.clone.rows_hbm) | copy-start | bytes 6291460
  8.2 22.5 %copy-start.4 = (bf16[512,1024]{1,0:T(8,128)(2,1)S(1)}, bf16[512,1024]{1,0:T(8,128)(2,1)}, u32[]{:S(2)}) copy-start(bf16[512,1024]{1,0:T(8,128)(2,1)} %constant.17.clone.low_ref) | copy-start | bytes 3145732
  8.2 22.5 %copy-start.5 = (bf16[512,1024]{1,0:T(8,128)(2,1)S(1)}, bf16[512,1024]{1,0:T(8,128)(2,1)}, u32[]{:S(2)}) copy-start(bf16[512,1024]{1,0:T(8,128)(2,1)} %constant.16.clone.high_ref) | copy-start | bytes 3145732
  8.2 22.5 %copy-start.6 = (bf16[512,512]{1,0:T(8,128)(2,1)S(1)}, bf16[512,512]{1,0:T(8,128)(2,1)}, u32[]{:S(2)}) copy-start(bf16[512,512]{1,0:T(8,128)(2,1)} %constant.15.clone.col_ref) | copy-start | bytes 1572868

commit v2 on v1

--- a/solution.py
+++ b/solution.py
@@ -27,6 +27,29 @@
 def forward_table(length):
     cos, sin = twiddles(np.arange(length), length, 1.0 / math.sqrt(length))
     return np.concatenate([cos, sin], 1).astype(np.float32).astype(BF16)
+
+
+@functools.lru_cache(maxsize=None)
+def row_table_of(length):
+    table, h = forward_table(length).T, P_SIZE // 2
+    rows = [table[:h], table[P_SIZE : P_SIZE + h], table[h : h + 1]]
+    return np.concatenate(rows + [np.zeros((15, length), BF16)], 0)
+
+
+@functools.lru_cache(maxsize=None)
+def unfold_tables(n):
+    p, h, width = P_SIZE, P_SIZE // 2, 2 * P_SIZE // n
+    own, flip, side, zero = np.eye(p), np.zeros((p, p)), np.zeros((p, h)), np.zeros((p, h))
+    flip[np.arange(1, p), p - np.arange(1, p)] = 1.0
+    side[np.arange(p), h - width + np.arange(p) % width] = 1.0
+    pick_re, pick_im = np.zeros((p, h)), np.zeros((p, h))
+    pick_re[0, 0] = pick_im[0, 1] = 1.0
+    real = np.block([[own, zero], [flip, pick_re], [np.zeros((p, p)), side]])
+    imag = np.block([[own, zero], [-flip, pick_im], [np.zeros((p, p)), side]])
+    back = np.zeros((p, h))
+    back[h - np.arange(1, h), np.arange(1, h)] = 1.0
+    back[h:, 0] = 1.0
+    return np.stack([real, imag]).astype(BF16), back.astype(BF16)
 
 
 @functools.lru_cache(maxsize=None)
@@ -56,8 +79,8 @@
 
 def spectrum_kernel(
     n_row, n_src, chunks,
-    mask_hbm, col_hbm, row_hbm, own_ref,
-    spec_ref, points_ref,
+    mask_hbm, col_hbm, row_hbm, own_shifts, own_weights,
+    spec_ref, shifts_ref, weights_ref,
     mask, col, row, half, part, send, arrived,
     load_sem, rs_send, rs_recv, ag_send, ag_recv, pt_send, pt_recv,
 ):
@@ -66,7 +89,7 @@
     me = row_id * n_src + src_id
     rows, cols = mask.shape
     piece = rows // chunks
-    per = P_SIZE // n
+    per = P_SIZE // 2 // n
 
     loads = [
         pltpu.make_async_copy(
@@ -105,9 +128,18 @@
         ).astype(jnp.bfloat16)
     loads[-1].wait()
     blocks = jnp.dot(row[...], half[...], preferred_element_type=jnp.float32)
-    p = P_SIZE
-    part[:, :p] = blocks[:p, :p] - blocks[p:, p:]
-    part[:, p:] = -blocks[:p, p:] - blocks[p:, :p]
+    p, h = P_SIZE, P_SIZE // 2
+    cos_re, cos_im = blocks[:h, :p], -blocks[:h, p:]
+    sin_re, sin_im = blocks[h:p, :p], -blocks[h:p, p:]
+    part[:, :p] = cos_re + sin_im
+    part[:, p : 2 * p] = cos_im - sin_re
+    lane = lax.broadcasted_iota(jnp.int32, (h, h), 1)
+    mirror_re, mirror_im = (cos_re - sin_im)[:, :1], (cos_im + sin_re)[:, :1]
+    part[:, 2 * p :] = jnp.where(lane == 0, mirror_re, jnp.where(lane == 1, mirror_im, 0.0))
+    middle = jnp.concatenate([blocks[p : p + 1, :p], -blocks[p : p + 1, p:]], 1)
+    width = 2 * p // n
+    for d in range(n):
+        part[pl.ds(d * per, 1), 2 * p + h - width :] = middle[:, d * width : (d + 1) * width]
     send[...] = part[...].astype(jnp.bfloat16)
 
     pl.semaphore_wait(barrier, n - 1)
@@ -124,14 +156,16 @@
         outgoing.append(copy)
     point_copies = []
     for k in range(1, n_src):
-        copy = pltpu.make_async_remote_copy(
-            src_ref=own_ref, dst_ref=points_ref.at[src_id],
-            send_sem=pt_send.at[k], recv_sem=pt_recv.at[k],
-            device_id={"src": lax.rem(src_id + k, n_src)}, device_id_type=MESH,
-        )
-        copy.start()
-        point_copies.append(copy)
-    points_ref[src_id] = own_ref[...]
+        for i, (own, everyone) in enumerate([(own_shifts, shifts_ref), (own_weights, weights_ref)]):
+            copy = pltpu.make_async_remote_copy(
+                src_ref=own, dst_ref=everyone.at[src_id],
+                send_sem=pt_send.at[i, k], recv_sem=pt_recv.at[i, k],
+                device_id={"src": lax.rem(src_id + k, n_src)}, device_id_type=MESH,
+            )
+            copy.start()
+            point_copies.append(copy)
+    shifts_ref[src_id] = own_shifts[...]
+    weights_ref[src_id] = own_weights[...]
 
     mine = pl.ds(pl.multiple_of(me * per, per), per)
     total = part[mine]
@@ -154,25 +188,45 @@
         copy.wait_send()
 
 
-def image_kernel(spec_ref, points, rows_hbm, col_ref, high_ref, low_ref, out_ref, rows, turned, halves, total, sem):
+def image_kernel(
+    spec_ref, shifts, weights, unfold_ref, back_ref, rows_hbm, col_ref, high_hbm, low_hbm,
+    out_ref, rows, high_ref, low_ref, turned, halves, total, sem,
+):
     n_src = lax.axis_size("src")
     me = lax.axis_index("row") * n_src + lax.axis_index("src")
     load = pltpu.make_async_copy(rows_hbm.at[me], rows, sem.at[0])
+    load_high = pltpu.make_async_copy(high_hbm, high_ref, sem.at[1])
+    load_low = pltpu.make_async_copy(low_hbm, low_ref, sem.at[2])
     load.start()
+    load_high.start()
+    load_low.start()
     p = P_SIZE
     block = out_ref.shape[0]
-    per = points.shape[1]
-    sources = points.shape[0] * per
-    turned[:, :p] = spec_ref[:, :p].astype(jnp.float32).T.astype(jnp.bfloat16)
-    turned[:, p:] = spec_ref[:, p:].astype(jnp.float32).T.astype(jnp.bfloat16)
+    per = weights.shape[2]
+    sources = n_src * per
+    h, width = p // 2, 2 * p // (NI // block)
+    lane = lax.broadcasted_iota(jnp.int32, (p, h), 1)
+    line = lax.broadcasted_iota(jnp.int32, (p, h), 0)
+    chunk = h // (NI // block)
+    for i in range(2):
+        kept = jnp.concatenate([spec_ref[:, i * p : (i + 1) * p], spec_ref[:, 2 * p :]], 1)
+        picked = lax.dot_general(
+            unfold_ref[i], kept, (((1,), (1,)), ((), ())), preferred_element_type=jnp.float32
+        )
+        holder = (i * p + line) // width * chunk
+        middle = jnp.where(lane == holder, picked[2 * p :], 0.0)
+        mirrored = jnp.concatenate([picked[p : 2 * p], middle], 1).astype(jnp.bfloat16)
+        upper = jnp.dot(mirrored, back_ref[...], preferred_element_type=jnp.float32)
+        turned[:, i * p : i * p + h] = picked[:p].astype(jnp.bfloat16)
+        turned[:, i * p + h : (i + 1) * p] = upper.astype(jnp.bfloat16)
     along_rows = lax.broadcasted_iota(jnp.int32, (p, p), 1) - p // 2
     along_cols = lax.broadcasted_iota(jnp.int32, (p, p), 0) - p // 2
     radius = p // 4
     load.wait()
 
     def first(s, carry):
-        down = along_rows + points[s // per, lax.rem(s, per), 0]
-        across = along_cols + points[s // per, lax.rem(s, per), 1]
+        down = along_rows + shifts[s // per, 0, lax.rem(s, per)]
+        across = along_cols + shifts[s // per, 1, lax.rem(s, per)]
         inside = down * down + across * across <= radius * radius
         pupil = jnp.where(inside, 1.0, 0.0).astype(jnp.bfloat16)
         passed = jnp.concatenate([turned[:, :p] * pupil, turned[:, p:] * pupil], 1)
@@ -186,12 +240,14 @@
     total[...] = jnp.zeros_like(total)
 
     def second(s, carry):
-        weight = points[s // per, lax.rem(s, per), 2].astype(jnp.float32) * (1.0 / sources)
+        weight = weights[s // per, 0, lax.rem(s, per)].astype(jnp.float32) * (1.0 / sources)
         e = jnp.dot(col_ref[...], halves[s], preferred_element_type=jnp.float32)
         total[...] += weight * (e[:, :block] * e[:, :block] + e[:, block:] * e[:, block:])
         return carry
 
     lax.fori_loop(0, sources, second, 0, unroll=2)
+    load_high.wait()
+    load_low.wait()
     summed = total[...].T
     top = summed.astype(jnp.bfloat16)
     rest = (summed - top.astype(jnp.float32)).astype(jnp.bfloat16)
@@ -205,63 +261,73 @@
 def body(n_row, n_src, mask_clip, source_shifts, source_weights):
     n = n_row * n_src
     rows, cols = mask_clip.shape
-    per = P_SIZE // n
-    own = jnp.concatenate([source_shifts, source_weights[:, None]], 1)
+    side = P_SIZE // 2
+    kept = (side, 2 * P_SIZE + side)
+    shifts, weights = source_shifts.T, source_weights[None, :]
     chunks = 4
     vmem = pl.BlockSpec(memory_space=pltpu.VMEM)
-    anywhere = pl.BlockSpec(memory_space=pl.ANY)
-    spec, points = pl.pallas_call(
+    smem = pl.BlockSpec(memory_space=pltpu.SMEM)
+    hbm = pl.BlockSpec(memory_space=pltpu.HBM)
+    spec, all_shifts, all_weights = pl.pallas_call(
         functools.partial(spectrum_kernel, n_row, n_src, chunks),
         out_shape=(
-            jax.ShapeDtypeStruct((P_SIZE, 2 * P_SIZE), jnp.bfloat16),
-            jax.ShapeDtypeStruct((n_src,) + own.shape, jnp.int32),
+            jax.ShapeDtypeStruct(kept, jnp.bfloat16),
+            jax.ShapeDtypeStruct((n_src,) + shifts.shape, jnp.int32),
+            jax.ShapeDtypeStruct((n_src,) + weights.shape, jnp.int32),
         ),
-        in_specs=[anywhere, anywhere, anywhere, vmem],
-        out_specs=(vmem, vmem),
+        in_specs=[hbm, hbm, hbm, vmem, vmem],
+        out_specs=(vmem, vmem, vmem),
         scratch_shapes=[
             pltpu.VMEM((rows, cols), jnp.bfloat16),
             pltpu.VMEM((cols, 2 * P_SIZE), jnp.bfloat16),
-            pltpu.VMEM((2 * P_SIZE, rows), jnp.bfloat16),
+            pltpu.VMEM((P_SIZE + 16, rows), jnp.bfloat16),
             pltpu.VMEM((rows, 2 * P_SIZE), jnp.bfloat16),
-            pltpu.VMEM((P_SIZE, 2 * P_SIZE), jnp.float32),
-            pltpu.VMEM((P_SIZE, 2 * P_SIZE), jnp.bfloat16),
-            pltpu.VMEM((n, per, 2 * P_SIZE), jnp.bfloat16),
+            pltpu.VMEM(kept, jnp.float32),
+            pltpu.VMEM(kept, jnp.bfloat16),
+            pltpu.VMEM((n, side // n, kept[1]), jnp.bfloat16),
             pltpu.SemaphoreType.DMA((chunks + 2,)),
             pltpu.SemaphoreType.DMA((n,)),
             pltpu.SemaphoreType.DMA((n,)),
             pltpu.SemaphoreType.DMA((n,)),
             pltpu.SemaphoreType.DMA((n,)),
-            pltpu.SemaphoreType.DMA((n_src,)),
-            pltpu.SemaphoreType.DMA((n_src,)),
+            pltpu.SemaphoreType.DMA((2, n_src)),
+            pltpu.SemaphoreType.DMA((2, n_src)),
         ],
         compiler_params=pltpu.CompilerParams(
-            collective_id=0, has_side_effects=True, vmem_limit_bytes=40 * 2**20
+            collective_id=0, has_side_effects=True, vmem_limit_bytes=62 * 2**20
         ),
         name="spectrum",
     )(
         mask_clip,
         jnp.asarray(forward_table(n_src * cols)),
-        jnp.asarray(np.ascontiguousarray(forward_table(n_row * rows).T)),
-        own,
+        jnp.asarray(row_table_of(n_row * rows)),
+        shifts,
+        weights,
     )
     row_table, col_table, high, low = inverse_tables(n)
+    unfold, back = unfold_tables(n)
     block = NI // n
-    sources = n_src * own.shape[0]
+    sources = n_src * source_weights.shape[0]
     return pl.pallas_call(
         image_kernel,
         out_shape=jax.ShapeDtypeStruct((block, NI), jnp.float32),
-        in_specs=[vmem, pl.BlockSpec(memory_space=pltpu.SMEM), anywhere, vmem, vmem, vmem],
+        in_specs=[vmem, smem, smem, vmem, vmem, hbm, vmem, hbm, hbm],
         out_specs=vmem,
         scratch_shapes=[
             pltpu.VMEM((2 * P_SIZE, 2 * block), jnp.bfloat16),
+            pltpu.VMEM((COARSE, NI), jnp.bfloat16),
+            pltpu.VMEM((COARSE, NI), jnp.bfloat16),
             pltpu.VMEM((P_SIZE, 2 * P_SIZE), jnp.bfloat16),
             pltpu.VMEM((sources, 2 * P_SIZE, 2 * block), jnp.bfloat16),
             pltpu.VMEM((COARSE, block), jnp.float32),
-            pltpu.SemaphoreType.DMA((1,)),
+            pltpu.SemaphoreType.DMA((3,)),
         ],
-        compiler_params=pltpu.CompilerParams(vmem_limit_bytes=40 * 2**20),
+        compiler_params=pltpu.CompilerParams(vmem_limit_bytes=62 * 2**20),
         name="image",
-    )(spec, points, jnp.asarray(row_table), jnp.asarray(col_table), jnp.asarray(high), jnp.asarray(low))
+    )(
+        spec, all_shifts, all_weights,
+        *map(jnp.asarray, (unfold, back, row_table, col_table, high, low)),
+    )
 
 
 def solution(mesh):

time: 39.4 us -> 30.4 us (0.77)
  local copies, waits for them, and re-layouts: 8.08 us -> 0 us
  Pallas kernels: 30.9 us -> 30.2 us
    unnamed x15 -> x0, local copies, waits for them, and re-layouts: 7.34 us -> none
    pallas_call x1, Pallas kernels: 22.5 us -> 20.2 us  [body(): pl.pallas_call(functools.partial(spectrum_kernel, n_row, n_src, chunks),...]
    pallas_call x1, Pallas kernels: 8.44 us -> 10 us  [body(): pl.pallas_call(image_kernel, out_shape=jax.ShapeDtypeStruct((block, NI),...]
    broadcast_in_dim x1 -> x0, local copies, waits for them, and re-layouts: 0.74 us -> none  [body(): own = jnp.concatenate([source_shifts, source_weights[:, None]], 1)]
where the time goes in v2:
time: 30.4 us; the launch traced here: 30.2 us
  Pallas kernels  30.2 us (99%)
    pallas_call x1, Pallas kernels, body(): pl.pallas_call(functools.partial(spectrum_kernel, n_row, n_src, chunks),...  20.2 us
    pallas_call x1, Pallas kernels, body(): pl.pallas_call(image_kernel, out_shape=jax.ShapeDtypeStruct((block, NI),...  10 us

profile of v2, /device:TPU:0, one launch (start us, length us, event | category | flops | bytes accessed | tf_op | source)
XLA Modules:
  0.0 30.2 jit_solution(13074769094618594736)
XLA Ops:
  0.0 20.2 %spectrum.1 = (bf16[128,640]{1,0:T(8,128)(2,1)}, s32[4,2,4]{2,1,0:T(2,128)}, s32[4,1,4]{2,1,0:T(1,128)}) custom-call(bf16[2048,1024]{1,0:T(8,128)(2,1)} %mask_hbm.1, bf16[4096,512]{1,0:T(8,128)(2,1)} %constant.16.clone.col_hbm, bf16[272,4096]{1,0:T(8,128)(2,1)} %constant.17.clone.row_hbm, s32[2,4]{1,0:T(2,128)} %bitcast.2, s32[1,4]{1,0:T(1,128)} %bitcast.3), custom_call_target="tpu_custom_call" | custom-call | tf_op jit(solution)/shard_map/spectrum/pallas_call | solution.py:271
  20.2 10.0 %image.1 = f32[128,1024]{1,0:T(8,128)} custom-call(bf16[128,640]{1,0:T(8,128)(2,1)} %get-tuple-element.8.spec_ref, s32[4,2,4]{2,1,0:T(2,128)} %get-tuple-element.9.shifts, s32[4,1,4]{2,1,0:T(1,128)} %get-tuple-element.10.weights, bf16[2,768,384]{2,1,0:T(8,128)(2,1)} %constant.18.clone.unfold_ref, bf16[256,128]{1,0:T(8,128)(2,1)} %constant.19.clone.back_ref, ...), custom_call_target="tpu_custom_call" | custom-call | tf_op jit(solution)/shard_map/image/pallas_call | solution.py:311

commit v3 on v2

--- a/solution.py
+++ b/solution.py
@@ -12,7 +12,7 @@
 
 P_SIZE = 256
 NI = 1024
-COARSE = 512
+COARSE = 384
 MESH = pl.DeviceIdType.MESH
 BF16 = ml_dtypes.bfloat16
 
@@ -33,7 +33,7 @@
 def row_table_of(length):
     table, h = forward_table(length).T, P_SIZE // 2
     rows = [table[:h], table[P_SIZE : P_SIZE + h], table[h : h + 1]]
-    return np.concatenate(rows + [np.zeros((15, length), BF16)], 0)
+    return np.concatenate(rows + [np.zeros((P_SIZE - 1, length), BF16)], 0)
 
 
 @functools.lru_cache(maxsize=None)
@@ -55,7 +55,8 @@
 @functools.lru_cache(maxsize=None)
 def inverse_tables(row_blocks):
     cos, sin = twiddles(np.arange(NI), NI, 1.0 / math.sqrt(P_SIZE))
-    cols = np.concatenate([cos, sin], 1)[:: NI // COARSE]
+    step = NI / COARSE
+    cols = np.concatenate(twiddles(np.arange(COARSE) * step, NI, 1.0 / math.sqrt(P_SIZE)), 1)
     block = NI // row_blocks
     rows = np.stack(
         [
@@ -67,10 +68,8 @@
     u = np.arange(-COARSE, COARSE + 1)
     ramp = np.clip((np.abs(u) - band) / (COARSE - 2 * band), 0.0, 1.0)
     gain = 0.5 + 0.5 * np.cos(math.pi * ramp)
-    offset = np.arange(NI)
-    kernel = (gain[None, :] * np.cos(2 * math.pi * offset[:, None] * u[None, :] / NI)).sum(1) / COARSE
-    step = NI // COARSE
-    spread = kernel[np.mod(np.arange(NI)[None, :] - step * np.arange(COARSE)[:, None], NI)]
+    offset = np.arange(NI)[None, :] - step * np.arange(COARSE)[:, None]
+    spread = sum(g * np.cos(2 * math.pi / NI * v * offset) for g, v in zip(gain, u)) / COARSE
     high = spread.astype(np.float32).astype(BF16)
     low = (spread - high.astype(np.float64)).astype(np.float32).astype(BF16)
     as_bf16 = lambda x: x.astype(np.float32).astype(BF16)
@@ -105,7 +104,7 @@
         )
     loads.append(
         pltpu.make_async_copy(
-            row_hbm.at[:, pl.ds(pl.multiple_of(row_id * rows, rows), rows)], row,
+            row_hbm.at[pl.ds(0, row.shape[0]), pl.ds(pl.multiple_of(row_id * rows, rows), rows)], row,
             load_sem.at[1 + chunks],
         )
     )
@@ -236,7 +235,7 @@
         halves[s, p:, block:] = k[:, :block]
         return carry
 
-    lax.fori_loop(0, sources, first, 0, unroll=2)
+    lax.fori_loop(0, sources, first, 0, unroll=16)
     total[...] = jnp.zeros_like(total)
 
     def second(s, carry):
@@ -245,7 +244,7 @@
         total[...] += weight * (e[:, :block] * e[:, :block] + e[:, block:] * e[:, block:])
         return carry
 
-    lax.fori_loop(0, sources, second, 0, unroll=2)
+    lax.fori_loop(0, sources, second, 0, unroll=16)
     load_high.wait()
     load_low.wait()
     summed = total[...].T

time: 30.4 us -> 27.2 us (0.89)
  Pallas kernels: 30.2 us -> 27.1 us
    pallas_call x1, Pallas kernels: 10 us -> 6.92 us  [body(): pl.pallas_call(image_kernel, out_shape=jax.ShapeDtypeStruct((block, NI),...]
where the time goes in v3:
time: 27.2 us; the launch traced here: 27.1 us
  Pallas kernels  27.1 us (100%)
    pallas_call x1, Pallas kernels, body(): pl.pallas_call(functools.partial(spectrum_kernel, n_row, n_src, chunks),...  20.2 us
    pallas_call x1, Pallas kernels, body(): pl.pallas_call(image_kernel, out_shape=jax.ShapeDtypeStruct((block, NI),...  6.92 us

profile of v3, /device:TPU:0, one launch (start us, length us, event | category | flops | bytes accessed | tf_op | source)
XLA Modules:
  0.0 27.1 jit_solution(17168409520913142693)
XLA Ops:
  0.0 20.2 %spectrum.1 = (bf16[128,640]{1,0:T(8,128)(2,1)}, s32[4,2,4]{2,1,0:T(2,128)}, s32[4,1,4]{2,1,0:T(1,128)}) custom-call(bf16[2048,1024]{1,0:T(8,128)(2,1)} %mask_hbm.1, bf16[4096,512]{1,0:T(8,128)(2,1)} %constant.16.clone.col_hbm, bf16[512,4096]{1,0:T(8,128)(2,1)} %constant.17.clone.row_hbm, s32[2,4]{1,0:T(2,128)} %bitcast.2, s32[1,4]{1,0:T(1,128)} %bitcast.3), custom_call_target="tpu_custom_call" | custom-call | tf_op jit(solution)/shard_map/spectrum/pallas_call | solution.py:270
  20.2 6.9 %image.1 = f32[128,1024]{1,0:T(8,128)} custom-call(bf16[128,640]{1,0:T(8,128)(2,1)} %get-tuple-element.8.spec_ref, s32[4,2,4]{2,1,0:T(2,128)} %get-tuple-element.9.shifts, s32[4,1,4]{2,1,0:T(1,128)} %get-tuple-element.10.weights, bf16[2,768,384]{2,1,0:T(8,128)(2,1)} %constant.18.clone.unfold_ref, bf16[256,128]{1,0:T(8,128)(2,1)} %constant.19.clone.back_ref, ...), custom_call_target="tpu_custom_call" | custom-call | tf_op jit(solution)/shard_map/image/pallas_call | solution.py:310

commit v4 on v3

--- a/solution.py
+++ b/solution.py
@@ -76,12 +76,14 @@
     return as_bf16(rows), as_bf16(cols), high, low
 
 
-def spectrum_kernel(
+def kernel(
     n_row, n_src, chunks,
     mask_hbm, col_hbm, row_hbm, own_shifts, own_weights,
-    spec_ref, shifts_ref, weights_ref,
+    unfold_hbm, back_hbm, rows_hbm, col_ref_hbm, total,
     mask, col, row, half, part, send, arrived,
-    load_sem, rs_send, rs_recv, ag_send, ag_recv, pt_send, pt_recv,
+    spec_ref, shifts_ref, weights_ref, shifts, weights,
+    unfold_ref, back_ref, image_rows, col_ref, pupils, turned, halves,
+    load_sem, table_sem, point_sem, rs_send, rs_recv, ag_send, ag_recv, pt_send, pt_recv,
 ):
     n = n_row * n_src
     row_id, src_id = lax.axis_index("row"), lax.axis_index("src")
@@ -110,6 +112,15 @@
     )
     for load in loads:
         load.start()
+    tables = [
+        pltpu.make_async_copy(there, here, table_sem.at[i])
+        for i, (there, here) in enumerate(
+            [
+                (unfold_hbm, unfold_ref), (back_hbm, back_ref), (rows_hbm.at[me], image_rows),
+                (col_ref_hbm, col_ref),
+            ]
+        )
+    ]
 
     def partner(k):
         other = lax.rem(me + k, n)
@@ -126,6 +137,8 @@
             mask[pl.ds(i * piece, piece)], col[...], preferred_element_type=jnp.float32
         ).astype(jnp.bfloat16)
     loads[-1].wait()
+    for table in tables:
+        table.start()
     blocks = jnp.dot(row[...], half[...], preferred_element_type=jnp.float32)
     p, h = P_SIZE, P_SIZE // 2
     cos_re, cos_im = blocks[:h, :p], -blocks[:h, p:]
@@ -142,17 +155,6 @@
     send[...] = part[...].astype(jnp.bfloat16)
 
     pl.semaphore_wait(barrier, n - 1)
-    outgoing = []
-    for k in range(1, n):
-        other, where = partner(k)
-        copy = pltpu.make_async_remote_copy(
-            src_ref=send.at[pl.ds(pl.multiple_of(other * per, per), per)],
-            dst_ref=arrived.at[k],
-            send_sem=rs_send.at[k], recv_sem=rs_recv.at[k],
-            device_id=where, device_id_type=MESH,
-        )
-        copy.start()
-        outgoing.append(copy)
     point_copies = []
     for k in range(1, n_src):
         for i, (own, everyone) in enumerate([(own_shifts, shifts_ref), (own_weights, weights_ref)]):
@@ -165,13 +167,47 @@
             point_copies.append(copy)
     shifts_ref[src_id] = own_shifts[...]
     weights_ref[src_id] = own_weights[...]
+    outgoing = []
+    for k in range(1, n):
+        other, where = partner(k)
+        copy = pltpu.make_async_remote_copy(
+            src_ref=send.at[pl.ds(pl.multiple_of(other * per, per), per)],
+            dst_ref=arrived.at[k],
+            send_sem=rs_send.at[k], recv_sem=rs_recv.at[k],
+            device_id=where, device_id_type=MESH,
+        )
+        copy.start()
+        outgoing.append(copy)
+    for copy in point_copies:
+        copy.wait_recv()
+    to_scalars = [
+        pltpu.make_async_copy(shifts_ref, shifts, point_sem.at[0]),
+        pltpu.make_async_copy(weights_ref, weights, point_sem.at[1]),
+    ]
+    for copy in to_scalars:
+        copy.start()
+    for copy in to_scalars:
+        copy.wait()
+    sources, count = pupils.shape[0], weights.shape[2]
+    along_rows = lax.broadcasted_iota(jnp.int32, (p, p), 1) - h
+    along_cols = lax.broadcasted_iota(jnp.int32, (p, p), 0) - h
+    radius = p // 4
+
+    def make_pupil(s, carry):
+        down = along_rows + shifts[s // count, 0, lax.rem(s, count)]
+        across = along_cols + shifts[s // count, 1, lax.rem(s, count)]
+        inside = down * down + across * across <= radius * radius
+        pupils[s] = jnp.where(inside, 1.0, 0.0).astype(jnp.bfloat16)
+        return carry
+
+    lax.fori_loop(0, sources, make_pupil, 0)
 
     mine = pl.ds(pl.multiple_of(me * per, per), per)
-    total = part[mine]
+    reduced = part[mine]
     for k, copy in enumerate(outgoing, 1):
         copy.wait_recv()
-        total = total + arrived[k].astype(jnp.float32)
-    spec_ref[mine] = total.astype(jnp.bfloat16)
+        reduced = reduced + arrived[k].astype(jnp.float32)
+    spec_ref[mine] = reduced.astype(jnp.bfloat16)
     gathered = []
     for k in range(1, n):
         copy = pltpu.make_async_remote_copy(
@@ -181,55 +217,32 @@
         )
         copy.start()
         gathered.append(copy)
-    for copy in point_copies + gathered:
+    for copy in gathered:
         copy.wait_recv()
     for copy in outgoing + point_copies + gathered:
         copy.wait_send()
 
-
-def image_kernel(
-    spec_ref, shifts, weights, unfold_ref, back_ref, rows_hbm, col_ref, high_hbm, low_hbm,
-    out_ref, rows, high_ref, low_ref, turned, halves, total, sem,
-):
-    n_src = lax.axis_size("src")
-    me = lax.axis_index("row") * n_src + lax.axis_index("src")
-    load = pltpu.make_async_copy(rows_hbm.at[me], rows, sem.at[0])
-    load_high = pltpu.make_async_copy(high_hbm, high_ref, sem.at[1])
-    load_low = pltpu.make_async_copy(low_hbm, low_ref, sem.at[2])
-    load.start()
-    load_high.start()
-    load_low.start()
-    p = P_SIZE
-    block = out_ref.shape[0]
-    per = weights.shape[2]
-    sources = n_src * per
-    h, width = p // 2, 2 * p // (NI // block)
+    for table in tables:
+        table.wait()
+    block = total.shape[1]
     lane = lax.broadcasted_iota(jnp.int32, (p, h), 1)
     line = lax.broadcasted_iota(jnp.int32, (p, h), 0)
-    chunk = h // (NI // block)
     for i in range(2):
         kept = jnp.concatenate([spec_ref[:, i * p : (i + 1) * p], spec_ref[:, 2 * p :]], 1)
         picked = lax.dot_general(
             unfold_ref[i], kept, (((1,), (1,)), ((), ())), preferred_element_type=jnp.float32
         )
-        holder = (i * p + line) // width * chunk
+        holder = (i * p + line) // width * per
         middle = jnp.where(lane == holder, picked[2 * p :], 0.0)
         mirrored = jnp.concatenate([picked[p : 2 * p], middle], 1).astype(jnp.bfloat16)
         upper = jnp.dot(mirrored, back_ref[...], preferred_element_type=jnp.float32)
         turned[:, i * p : i * p + h] = picked[:p].astype(jnp.bfloat16)
         turned[:, i * p + h : (i + 1) * p] = upper.astype(jnp.bfloat16)
-    along_rows = lax.broadcasted_iota(jnp.int32, (p, p), 1) - p // 2
-    along_cols = lax.broadcasted_iota(jnp.int32, (p, p), 0) - p // 2
-    radius = p // 4
-    load.wait()
 
     def first(s, carry):
-        down = along_rows + shifts[s // per, 0, lax.rem(s, per)]
-        across = along_cols + shifts[s // per, 1, lax.rem(s, per)]
-        inside = down * down + across * across <= radius * radius
-        pupil = jnp.where(inside, 1.0, 0.0).astype(jnp.bfloat16)
+        pupil = pupils[s]
         passed = jnp.concatenate([turned[:, :p] * pupil, turned[:, p:] * pupil], 1)
-        k = jnp.dot(passed, rows[...], preferred_element_type=jnp.float32).astype(jnp.bfloat16)
+        k = jnp.dot(passed, image_rows[...], preferred_element_type=jnp.float32).astype(jnp.bfloat16)
         halves[s, :p] = k
         halves[s, p:, :block] = -k[:, block:]
         halves[s, p:, block:] = k[:, :block]
@@ -239,14 +252,15 @@
     total[...] = jnp.zeros_like(total)
 
     def second(s, carry):
-        weight = weights[s // per, 0, lax.rem(s, per)].astype(jnp.float32) * (1.0 / sources)
+        weight = weights[s // count, 0, lax.rem(s, count)].astype(jnp.float32) * (1.0 / sources)
         e = jnp.dot(col_ref[...], halves[s], preferred_element_type=jnp.float32)
         total[...] += weight * (e[:, :block] * e[:, :block] + e[:, block:] * e[:, block:])
         return carry
 
     lax.fori_loop(0, sources, second, 0, unroll=16)
-    load_high.wait()
-    load_low.wait()
+
+
+def spread_kernel(total, high_ref, low_ref, out_ref):
     summed = total[...].T
     top = summed.astype(jnp.bfloat16)
     rest = (summed - top.astype(jnp.float32)).astype(jnp.bfloat16)
@@ -265,17 +279,17 @@
     shifts, weights = source_shifts.T, source_weights[None, :]
     chunks = 4
     vmem = pl.BlockSpec(memory_space=pltpu.VMEM)
-    smem = pl.BlockSpec(memory_space=pltpu.SMEM)
     hbm = pl.BlockSpec(memory_space=pltpu.HBM)
-    spec, all_shifts, all_weights = pl.pallas_call(
-        functools.partial(spectrum_kernel, n_row, n_src, chunks),
-        out_shape=(
-            jax.ShapeDtypeStruct(kept, jnp.bfloat16),
-            jax.ShapeDtypeStruct((n_src,) + shifts.shape, jnp.int32),
-            jax.ShapeDtypeStruct((n_src,) + weights.shape, jnp.int32),
-        ),
-        in_specs=[hbm, hbm, hbm, vmem, vmem],
-        out_specs=(vmem, vmem, vmem),
+    unfold, back = unfold_tables(n)
+    row_table, col_table, high, low = inverse_tables(n)
+    block = NI // n
+    count = source_weights.shape[0]
+    sources = n_src * count
+    total = pl.pallas_call(
+        functools.partial(kernel, n_row, n_src, chunks),
+        out_shape=jax.ShapeDtypeStruct((COARSE, block), jnp.float32),
+        in_specs=[hbm] * 3 + [vmem] * 2 + [hbm] * 4,
+        out_specs=vmem,
         scratch_shapes=[
             pltpu.VMEM((rows, cols), jnp.bfloat16),
             pltpu.VMEM((cols, 2 * P_SIZE), jnp.bfloat16),
@@ -284,7 +298,21 @@
             pltpu.VMEM(kept, jnp.float32),
             pltpu.VMEM(kept, jnp.bfloat16),
             pltpu.VMEM((n, side // n, kept[1]), jnp.bfloat16),
+            pltpu.VMEM(kept, jnp.bfloat16),
+            pltpu.VMEM((n_src, 2, count), jnp.int32),
+            pltpu.VMEM((n_src, 1, count), jnp.int32),
+            pltpu.SMEM((n_src, 2, count), jnp.int32),
+            pltpu.SMEM((n_src, 1, count), jnp.int32),
+            pltpu.VMEM(unfold.shape, jnp.bfloat16),
+            pltpu.VMEM(back.shape, jnp.bfloat16),
+            pltpu.VMEM((2 * P_SIZE, 2 * block), jnp.bfloat16),
+            pltpu.VMEM(col_table.shape, jnp.bfloat16),
+            pltpu.VMEM((sources, P_SIZE, P_SIZE), jnp.bfloat16),
+            pltpu.VMEM((P_SIZE, 2 * P_SIZE), jnp.bfloat16),
+            pltpu.VMEM((sources, 2 * P_SIZE, 2 * block), jnp.bfloat16),
             pltpu.SemaphoreType.DMA((chunks + 2,)),
+            pltpu.SemaphoreType.DMA((4,)),
+            pltpu.SemaphoreType.DMA((2,)),
             pltpu.SemaphoreType.DMA((n,)),
             pltpu.SemaphoreType.DMA((n,)),
             pltpu.SemaphoreType.DMA((n,)),
@@ -295,38 +323,23 @@
         compiler_params=pltpu.CompilerParams(
             collective_id=0, has_side_effects=True, vmem_limit_bytes=62 * 2**20
         ),
-        name="spectrum",
+        name="image",
     )(
         mask_clip,
         jnp.asarray(forward_table(n_src * cols)),
         jnp.asarray(row_table_of(n_row * rows)),
         shifts,
         weights,
-    )
-    row_table, col_table, high, low = inverse_tables(n)
-    unfold, back = unfold_tables(n)
-    block = NI // n
-    sources = n_src * source_weights.shape[0]
+        *map(jnp.asarray, (unfold, back, row_table, col_table)),
+    )
     return pl.pallas_call(
-        image_kernel,
+        spread_kernel,
         out_shape=jax.ShapeDtypeStruct((block, NI), jnp.float32),
-        in_specs=[vmem, smem, smem, vmem, vmem, hbm, vmem, hbm, hbm],
+        in_specs=[vmem] * 3,
         out_specs=vmem,
-        scratch_shapes=[
-            pltpu.VMEM((2 * P_SIZE, 2 * block), jnp.bfloat16),
-            pltpu.VMEM((COARSE, NI), jnp.bfloat16),
-            pltpu.VMEM((COARSE, NI), jnp.bfloat16),
-            pltpu.VMEM((P_SIZE, 2 * P_SIZE), jnp.bfloat16),
-            pltpu.VMEM((sources, 2 * P_SIZE, 2 * block), jnp.bfloat16),
-            pltpu.VMEM((COARSE, block), jnp.float32),
-            pltpu.SemaphoreType.DMA((3,)),
-        ],
         compiler_params=pltpu.CompilerParams(vmem_limit_bytes=62 * 2**20),
-        name="image",
-    )(
-        spec, all_shifts, all_weights,
-        *map(jnp.asarray, (unfold, back, row_table, col_table, high, low)),
-    )
+        name="spread",
+    )(total, jnp.asarray(high), jnp.asarray(low))
 
 
 def solution(mesh):

time: 27.2 us -> 26.9 us (0.989)
  Pallas kernels: 27.1 us -> 26.7 us
    pallas_call x2, Pallas kernels: 27.1 us -> 26.7 us  [the longest x1 23.8 us: body(): pl.pallas_call(functools.partial(kernel, n_row, n_src, chunks), out_shape...]
where the time goes in v4:
time: 26.9 us; the launch traced here: 26.7 us
  Pallas kernels  26.7 us (99%)
    pallas_call x1, Pallas kernels, body(): pl.pallas_call(functools.partial(kernel, n_row, n_src, chunks), out_shape...  23.8 us
    pallas_call x1, Pallas kernels, body(): pl.pallas_call(spread_kernel, out_shape=jax.ShapeDtypeStruct((block, NI),...  2.85 us

profile of v4, /device:TPU:0, one launch (start us, length us, event | category | flops | bytes accessed | tf_op | source)
XLA Modules:
  0.0 26.7 jit_solution(13885148827013231340)
XLA Ops:
  0.0 23.8 %image.1.total = f32[384,128]{1,0:T(8,128)} custom-call(bf16[2048,1024]{1,0:T(8,128)(2,1)} %mask_hbm.1, bf16[4096,512]{1,0:T(8,128)(2,1)} %constant.16.clone.col_hbm, bf16[512,4096]{1,0:T(8,128)(2,1)} %constant.17.clone.row_hbm, s32[2,4]{1,0:T(2,128)} %bitcast.2, s32[1,4]{1,0:T(1,128)} %bitcast.3, bf16[2,768,384]{2,1,0:T(8,128)(2,1)} %constant.18.clone.unfold_hbm, ...), custom_call_target="tpu_custom_call" | custom-call | tf_op jit(solution)/shard_map/image/pallas_call | solution.py:288
  23.8 2.8 %spread.1 = f32[128,1024]{1,0:T(8,128)} custom-call(f32[384,128]{1,0:T(8,128)} %image.1.total, bf16[384,1024]{1,0:T(8,128)(2,1)} %constant.22.clone.high_ref, bf16[384,1024]{1,0:T(8,128)(2,1)} %constant.23.clone.low_ref), custom_call_target="tpu_custom_call" | custom-call | tf_op jit(solution)/shard_map/spread/pallas_call | solution.py:335

commit v5 on v4

--- a/solution.py
+++ b/solution.py
@@ -277,7 +277,7 @@
     side = P_SIZE // 2
     kept = (side, 2 * P_SIZE + side)
     shifts, weights = source_shifts.T, source_weights[None, :]
-    chunks = 4
+    chunks = 8
     vmem = pl.BlockSpec(memory_space=pltpu.VMEM)
     hbm = pl.BlockSpec(memory_space=pltpu.HBM)
     unfold, back = unfold_tables(n)

time: 26.9 us -> 27.4 us (1.019)
  Pallas kernels: 26.7 us -> 27.2 us
    pallas_call x1, Pallas kernels: 23.8 us -> 24.4 us  [body(): pl.pallas_call(functools.partial(kernel, n_row, n_src, chunks), out_shape...]
where the time goes in v5:
time: 27.4 us; the launch traced here: 27.2 us
  Pallas kernels  27.2 us (99%)
    pallas_call x1, Pallas kernels, body(): pl.pallas_call(functools.partial(kernel, n_row, n_src, chunks), out_shape...  24.4 us
    pallas_call x1, Pallas kernels, body(): pl.pallas_call(spread_kernel, out_shape=jax.ShapeDtypeStruct((block, NI),...  2.85 us

profile of v5, /device:TPU:0, one launch (start us, length us, event | category | flops | bytes accessed | tf_op | source)
XLA Modules:
  0.0 27.2 jit_solution(9088841115808703463)
XLA Ops:
  0.0 24.4 %image.1.total = f32[384,128]{1,0:T(8,128)} custom-call(bf16[2048,1024]{1,0:T(8,128)(2,1)} %mask_hbm.1, bf16[4096,512]{1,0:T(8,128)(2,1)} %constant.16.clone.col_hbm, bf16[512,4096]{1,0:T(8,128)(2,1)} %constant.17.clone.row_hbm, s32[2,4]{1,0:T(2,128)} %bitcast.2, s32[1,4]{1,0:T(1,128)} %bitcast.3, bf16[2,768,384]{2,1,0:T(8,128)(2,1)} %constant.18.clone.unfold_hbm, ...), custom_call_target="tpu_custom_call" | custom-call | tf_op jit(solution)/shard_map/image/pallas_call | solution.py:288
  24.4 2.9 %spread.1 = f32[128,1024]{1,0:T(8,128)} custom-call(f32[384,128]{1,0:T(8,128)} %image.1.total, bf16[384,1024]{1,0:T(8,128)(2,1)} %constant.22.clone.high_ref, bf16[384,1024]{1,0:T(8,128)(2,1)} %constant.23.clone.low_ref), custom_call_target="tpu_custom_call" | custom-call | tf_op jit(solution)/shard_map/spread/pallas_call | solution.py:335
